TPU v7x, 32 devices: a whole 2x2x4 slice. The times are simulated.
32 devices in a mesh: dp: 2 (over core), expert: 4 (over z), tensor: 4 (over y, x).
Axes of the slice: x: 2, y: 2, z: 4, core: 2. Of those that a mesh axis runs over, the one named last changes fastest.
Arguments:
- tokens: bfloat16 [12288, 1024], P(('dp', 'expert', 'tensor')), may hold values from -6 to 6
- segments: int32 [12288], P(('dp', 'expert', 'tensor')), may hold values from 0 to 1535, as said below
- routes: int32 [12288, 8], P(('dp', 'expert', 'tensor')), may hold values from 0 to 31, all different within a row; in each aligned block of 384 rows (0 to 383, 384 to 767, ...) at most 128 rows name the same one
- norm_one: float32 [1024], replicated, may hold values from 0.1 to 1.9
- w_query: bfloat16 [1024, 1024], P(None, 'tensor'), may hold values from -0.1875 to 0.1875
- w_key: bfloat16 [1024, 512], P(None, 'tensor'), may hold values from -0.1875 to 0.1875
- w_value: bfloat16 [1024, 512], P(None, 'tensor'), may hold values from -0.1875 to 0.1875
- w_out: bfloat16 [1024, 1024], P('tensor'), may hold values from -0.5 to 0.5
- norm_two: float32 [1024], replicated, may hold values from 0.1 to 1.9
- w_router: bfloat16 [1024, 32], replicated, may hold values from -0.09375 to 0.09375
- w_gate: bfloat16 [32, 1024, 512], P('expert', None, 'tensor'), may hold values from -0.1875 to 0.1875
- w_up: bfloat16 [32, 1024, 512], P('expert', None, 'tensor'), may hold values from -0.1875 to 0.1875
- w_down: bfloat16 [32, 512, 1024], P('expert', 'tensor'), may hold values from -1 to 1
- cotangent: bfloat16 [12288, 1024], P(('dp', 'expert', 'tensor')), may hold values from -6 to 6
Outputs:
- block_out: bfloat16 [12288, 1024], P(('dp', 'expert', 'tensor'))
- grad_tokens: float32 [12288, 1024], P(('dp', 'expert', 'tensor'))
- grad_norm_one: float32 [1024], replicated
- grad_query: float32 [1024, 1024], P(None, 'tensor')
- grad_key: float32 [1024, 512], P(None, 'tensor')
- grad_value: float32 [1024, 512], P(None, 'tensor')
- grad_out: float32 [1024, 1024], P('tensor')
- grad_norm_two: float32 [1024], replicated
- grad_router: float32 [1024, 32], replicated
- grad_gate: float32 [32, 1024, 512], P('expert', None, 'tensor')
- grad_up: float32 [32, 1024, 512], P('expert', None, 'tensor')
- grad_down: float32 [32, 512, 1024], P('expert', 'tensor')
Inputs may be any that keep to these rules, and one draw needn't show every extreme that they name: `segments`: within each sequence of 1536 tokens the segment numbers start at 0 and never fall; the last segment of every sequence is numbered 1536 - 1; in every sequence one segment begins among its first 384 tokens and ends among its last 384. `routes`: each row names 8 different experts. Among the rows of one device no expert is named by more than 128 rows, a bound that some block reaches.
All inputs are finite; a program needn't handle non-finite values.
Results may differ from a plain program's by a relative error of at most 0.023.
Values may be sent and summed in bfloat16 or wider, within the bound.
A program may use at most 256 MiB of HBM per device.

v0:
```python
import jax
import jax.numpy as jnp
from jax import lax
from jax.sharding import PartitionSpec as P

HEAD = 64
TOP = 8
CAP = 128


epsilon = 1e-06
highest = lax.Precision.HIGHEST


def rms_norm(features, gain_vec):
    return (
        features
        * lax.rsqrt(jnp.mean(features * features, axis=-1, keepdims=True) + epsilon)
        * gain_vec
    )


def rotate(vectors, places):
    half_dim = vectors.shape[-1] // 2
    frequency = 10000.0 ** (-jnp.arange(half_dim, dtype=jnp.float32) / half_dim)
    angles = places.astype(jnp.float32)[:, None] * frequency[None, :]
    cosine = jnp.cos(angles)[:, None, :]
    sine_part = jnp.sin(angles)[:, None, :]
    front_half = vectors[..., :half_dim]
    back_half = vectors[..., half_dim:]
    return jnp.concatenate(
        [front_half * cosine - back_half * sine_part, back_half * cosine + front_half * sine_part],
        axis=-1,
    )


def contract_rows(left_in, right_in):
    return lax.dot_general(
        left_in, right_in, (((0,), (0,)), ((), ())), preferred_element_type=jnp.float32
    )


def contract_cols(left_in, right_in):
    return lax.dot_general(
        left_in, right_in, (((1,), (1,)), ((), ())), preferred_element_type=jnp.float32
    )


def to_owners(buffer):
    return lax.all_to_all(buffer, "expert", split_axis=0, concat_axis=0, tiled=True)


def to_sources(buffer):
    return lax.all_to_all(buffer, "expert", split_axis=0, concat_axis=0, tiled=True)


def body(
    tokens,
    segments,
    routes,
    norm_one,
    w_query,
    w_key,
    w_value,
    w_out,
    norm_two,
    w_router,
    w_gate,
    w_up,
    w_down,
    cotangent,
):
    local_rows = tokens.shape[0]
    model_width = tokens.shape[1]
    head_local = w_query.shape[1] // HEAD
    kv_local = w_key.shape[1] // HEAD
    group_size = head_local // kv_local
    expert_local = w_gate.shape[0]
    owner_count = lax.axis_size("expert")
    experts_all = expert_local * owner_count
    capacity = CAP
    score_scale = HEAD ** (-0.5)
    inputs = tokens.astype(jnp.float32)
    normed_one, norm_back_one = jax.vjp(rms_norm, inputs, norm_one)
    normed = normed_one.astype(jnp.bfloat16)
    normed_all, segs_all = (
        lax.all_gather(normed, "tensor", axis=0, tiled=True),
        lax.all_gather(segments, "tensor", axis=0, tiled=True),
    )
    length = normed_all.shape[0]
    places = jnp.arange(length, dtype=jnp.int32)
    query_raw = jnp.dot(normed_all, w_query, preferred_element_type=jnp.float32).reshape(
        length, head_local, HEAD
    )
    key_raw = jnp.dot(normed_all, w_key, preferred_element_type=jnp.float32).reshape(
        length, kv_local, HEAD
    )
    query_turned, rope_query = jax.vjp(lambda vectors: rotate(vectors, places), query_raw)
    key_turned, rope_key = jax.vjp(lambda vectors: rotate(vectors, places), key_raw)
    key_rows = key_turned.astype(jnp.bfloat16)
    value_rows = (
        jnp.dot(normed_all, w_value, preferred_element_type=jnp.float32)
        .astype(jnp.bfloat16)
        .reshape(length, kv_local, HEAD)
    )
    block_count = max(1, length // 512)
    block_rows = length // block_count
    block_places = places.reshape(block_count, block_rows)
    block_segs = segs_all.reshape(block_count, block_rows)
    block_queries = query_turned.astype(jnp.bfloat16).reshape(
        block_count, block_rows, kv_local, group_size, HEAD
    )

    def allowed_mask(query_places, query_segs):
        return (places[None, :] <= query_places[:, None]) & (
            segs_all[None, :] == query_segs[:, None]
        )

    def attend(pieces):
        query_block, query_places, query_segs = pieces
        scores = (
            jnp.einsum("qkgd,skd->kgqs", query_block, key_rows, preferred_element_type=jnp.float32)
            * score_scale
        )
        masked = jnp.where(allowed_mask(query_places, query_segs), scores, -1e30)
        largest = jnp.max(masked, axis=-1, keepdims=True)
        weights = jnp.exp(masked - largest)
        row_total = jnp.sum(weights, axis=-1, keepdims=True)
        prob_rows = (weights / row_total).astype(jnp.bfloat16)
        mixed_block = jnp.einsum(
            "kgqs,skd->qkgd", prob_rows, value_rows, preferred_element_type=jnp.float32
        )
        return (mixed_block, (largest + jnp.log(row_total))[..., 0])

    mixed_heads, log_totals = lax.map(attend, (block_queries, block_places, block_segs))
    mixed_heads = mixed_heads.reshape(length, head_local * HEAD).astype(jnp.bfloat16)
    attention = lax.psum_scatter(
        jnp.dot(mixed_heads, w_out, preferred_element_type=jnp.float32).astype(jnp.bfloat16),
        "tensor",
        scatter_dimension=0,
        tiled=True,
    ).astype(jnp.float32)
    hidden = inputs + attention
    normed_two, norm_back_two = jax.vjp(rms_norm, hidden, norm_two)
    routed = normed_two.astype(jnp.bfloat16)
    logits = jnp.dot(routed, w_router, preferred_element_type=jnp.float32)
    route_onehot = (
        routes[:, :, None] == jnp.arange(experts_all, dtype=jnp.int32)[None, None, :]
    ).astype(jnp.float32)
    chosen = jnp.sum(route_onehot * logits[:, None, :], axis=-1)
    gate_probs = jax.nn.softmax(chosen, axis=-1)
    route_flat = routes.reshape(-1)
    expert_marks = (
        route_flat[:, None] == jnp.arange(experts_all, dtype=jnp.int32)[None, :]
    ).astype(jnp.int32)
    slot_ranks = jnp.sum((jnp.cumsum(expert_marks, axis=0) - expert_marks) * expert_marks, axis=1)
    slot_index = route_flat * capacity + slot_ranks
    token_of_entry = jnp.arange(route_flat.shape[0], dtype=jnp.int32) // TOP
    send_rows = (
        jnp.zeros((experts_all * capacity, model_width), jnp.bfloat16)
        .at[slot_index]
        .set(routed[token_of_entry])
    )
    expert_in = to_owners(send_rows.reshape(owner_count, expert_local, capacity, model_width))
    gate_matrix, up_matrix, down_matrix = (
        lax.all_gather(w_gate, "tensor", axis=2, tiled=True),
        lax.all_gather(w_up, "tensor", axis=2, tiled=True),
        lax.all_gather(w_down, "tensor", axis=1, tiled=True),
    )
    gate_val = jnp.einsum(
        "nlcd,ldf->nlcf", expert_in, gate_matrix, preferred_element_type=jnp.float32
    )
    up_val = jnp.einsum("nlcd,ldf->nlcf", expert_in, up_matrix, preferred_element_type=jnp.float32)
    inner_full, silu_back = jax.vjp(
        lambda left_in, right_in: jax.nn.silu(left_in) * right_in, gate_val, up_val
    )
    inner_rows = inner_full.astype(jnp.bfloat16)
    results = jnp.einsum(
        "nlcf,lfd->nlcd", inner_rows, down_matrix, preferred_element_type=jnp.float32
    )
    returned = to_sources(results.astype(jnp.bfloat16)).reshape(experts_all * capacity, model_width)
    outputs = returned[slot_index].reshape(local_rows, TOP, model_width).astype(jnp.float32)
    block_out = hidden + jnp.sum(gate_probs[:, :, None] * outputs, axis=1)
    upstream = cotangent.astype(jnp.float32)
    gate_grad = jnp.sum(upstream[:, None, :] * outputs, axis=-1)
    out_back = (
        (gate_probs[:, :, None] * upstream[:, None, :])
        .astype(jnp.bfloat16)
        .reshape(-1, model_width)
    )
    send_back = (
        jnp.zeros((experts_all * capacity, model_width), jnp.bfloat16).at[slot_index].set(out_back)
    )
    grad_in = to_owners(send_back.reshape(owner_count, expert_local, capacity, model_width))
    inner_grad = jnp.einsum(
        "nlcd,lfd->nlcf", grad_in, down_matrix, preferred_element_type=jnp.float32
    )
    down_grad = jnp.einsum(
        "nlcf,nlcd->lfd", inner_rows, grad_in, preferred_element_type=jnp.float32
    )
    gate_back, up_back = silu_back(inner_grad)
    gate_back = gate_back.astype(jnp.bfloat16)
    up_back = up_back.astype(jnp.bfloat16)
    gate_wgrad = jnp.einsum(
        "nlcd,nlcf->ldf", expert_in, gate_back, preferred_element_type=jnp.float32
    )
    up_wgrad = jnp.einsum("nlcd,nlcf->ldf", expert_in, up_back, preferred_element_type=jnp.float32)
    row_grads = jnp.einsum(
        "nlcf,ldf->nlcd", gate_back, gate_matrix, preferred_element_type=jnp.float32
    ) + jnp.einsum("nlcf,ldf->nlcd", up_back, up_matrix, preferred_element_type=jnp.float32)
    gate_local, up_local, down_local = (
        lax.psum_scatter(
            gate_wgrad.astype(jnp.bfloat16), "tensor", scatter_dimension=2, tiled=True
        ).astype(jnp.float32),
        lax.psum_scatter(
            up_wgrad.astype(jnp.bfloat16), "tensor", scatter_dimension=2, tiled=True
        ).astype(jnp.float32),
        lax.psum_scatter(
            down_grad.astype(jnp.bfloat16), "tensor", scatter_dimension=1, tiled=True
        ).astype(jnp.float32),
    )
    row_back = to_sources(row_grads.astype(jnp.bfloat16)).reshape(
        experts_all * capacity, model_width
    )
    routed_grad = jnp.sum(
        row_back[slot_index].reshape(local_rows, TOP, model_width).astype(jnp.float32), axis=1
    )
    chosen_grad = gate_probs * (gate_grad - jnp.sum(gate_probs * gate_grad, axis=-1, keepdims=True))
    logit_grad = jnp.sum(route_onehot * chosen_grad[:, :, None], axis=1)
    router_float = w_router.astype(jnp.float32)
    routed_grad = routed_grad + lax.dot_general(
        logit_grad, router_float, (((1,), (1,)), ((), ())), precision=highest
    )
    router_grad = lax.dot_general(
        routed.astype(jnp.float32), logit_grad, (((0,), (0,)), ((), ())), precision=highest
    )
    hidden_part, norm_two_grad = norm_back_two(routed_grad)
    hidden_grad = upstream + hidden_part
    attn_grad = hidden_grad.astype(jnp.bfloat16)
    attn_all = lax.all_gather(attn_grad, "tensor", axis=0, tiled=True)
    out_wgrad = contract_rows(mixed_heads, attn_all)
    mixed_grad = (
        contract_cols(attn_all, w_out)
        .astype(jnp.bfloat16)
        .reshape(block_count, block_rows, kv_local, group_size, HEAD)
    )

    def back_block(carry_pair, pieces):
        key_acc, value_acc = carry_pair
        query_block, grad_block, query_places, query_segs, log_block = pieces
        scores = (
            jnp.einsum("qkgd,skd->kgqs", query_block, key_rows, preferred_element_type=jnp.float32)
            * score_scale
        )
        masked = jnp.where(allowed_mask(query_places, query_segs), scores, -1e30)
        prob_full = jnp.exp(masked - log_block[..., None])
        prob_grad = jnp.einsum(
            "qkgd,skd->kgqs", grad_block, value_rows, preferred_element_type=jnp.float32
        )
        value_acc = value_acc + jnp.einsum(
            "kgqs,qkgd->skd",
            prob_full.astype(jnp.bfloat16),
            grad_block,
            preferred_element_type=jnp.float32,
        )
        centred = jnp.sum(prob_full * prob_grad, axis=-1, keepdims=True)
        score_grad = (prob_full * (prob_grad - centred)).astype(jnp.bfloat16)
        query_grad = (
            jnp.einsum("kgqs,skd->qkgd", score_grad, key_rows, preferred_element_type=jnp.float32)
            * score_scale
        )
        key_acc = (
            key_acc
            + jnp.einsum(
                "kgqs,qkgd->skd", score_grad, query_block, preferred_element_type=jnp.float32
            )
            * score_scale
        )
        return ((key_acc, value_acc), query_grad)

    zero_keys = jnp.zeros((length, kv_local, HEAD), jnp.float32)
    carry_pair, query_grads = lax.scan(
        back_block,
        (zero_keys, zero_keys),
        (block_queries, mixed_grad, block_places, block_segs, log_totals),
    )
    key_grad, value_grad = carry_pair
    (query_raw_grad,) = rope_query(query_grads.reshape(length, head_local, HEAD))
    (key_raw_grad,) = rope_key(key_grad)
    query_low = query_raw_grad.reshape(length, head_local * HEAD).astype(jnp.bfloat16)
    key_low = key_raw_grad.reshape(length, kv_local * HEAD).astype(jnp.bfloat16)
    value_low = value_grad.reshape(length, kv_local * HEAD).astype(jnp.bfloat16)
    query_wgrad = contract_rows(normed_all, query_low)
    key_wgrad = contract_rows(normed_all, key_low)
    value_wgrad = contract_rows(normed_all, value_low)
    normed_grad = lax.psum_scatter(
        (
            contract_cols(query_low, w_query)
            + contract_cols(key_low, w_key)
            + contract_cols(value_low, w_value)
        ).astype(jnp.bfloat16),
        "tensor",
        scatter_dimension=0,
        tiled=True,
    ).astype(jnp.float32)
    input_part, norm_one_grad = norm_back_one(normed_grad)
    input_grad = hidden_grad + input_part
    norm_one_grad, norm_two_grad, router_grad = (
        lax.psum(norm_one_grad.astype(jnp.bfloat16), "tensor").astype(jnp.float32),
        lax.psum(norm_two_grad.astype(jnp.bfloat16), "tensor").astype(jnp.float32),
        lax.psum(router_grad.astype(jnp.bfloat16), "tensor").astype(jnp.float32),
    )
    summed_layer = lax.psum(
        (query_wgrad, key_wgrad, value_wgrad, out_wgrad, norm_one_grad, norm_two_grad, router_grad),
        ("dp", "expert"),
    )
    summed_expert = (
        lax.psum(gate_local.astype(jnp.bfloat16), "dp").astype(jnp.float32),
        lax.psum(up_local.astype(jnp.bfloat16), "dp").astype(jnp.float32),
        lax.psum(down_local.astype(jnp.bfloat16), "dp").astype(jnp.float32),
    )
    return (
        block_out.astype(jnp.bfloat16),
        input_grad,
        summed_layer[4],
        summed_layer[0],
        summed_layer[1],
        summed_layer[2],
        summed_layer[3],
        summed_layer[5],
        summed_layer[6],
        summed_expert[0],
        summed_expert[1],
        summed_expert[2],
    )


def solution(mesh):
    placed = (
        P(("dp", "expert", "tensor"), None),
        P(("dp", "expert", "tensor")),
        P(("dp", "expert", "tensor"), None),
        P(),
        P(None, "tensor"),
        P(None, "tensor"),
        P(None, "tensor"),
        P("tensor", None),
        P(),
        P(),
        P("expert", None, "tensor"),
        P("expert", None, "tensor"),
        P("expert", "tensor", None),
        P(("dp", "expert", "tensor"), None),
    )
    return jax.shard_map(
        body,
        mesh=mesh,
        in_specs=placed,
        out_specs=(
            P(("dp", "expert", "tensor"), None),
            P(("dp", "expert", "tensor"), None),
            P(),
            P(None, "tensor"),
            P(None, "tensor"),
            P(None, "tensor"),
            P("tensor", None),
            P(),
            P(),
            P("expert", None, "tensor"),
            P("expert", None, "tensor"),
            P("expert", "tensor", None),
        ),
        check_vma=False,
    )
```

profile of v0, /device:TPU:0, one launch (start us, length us, event | category | flops | bytes accessed | tf_op | source)
XLA Modules:
  0.0 1447.1 jit_solution(17927967485617205902)
XLA Ops:
  23.2 35.7 %all-gather.7.cloned.1.call-done = bf16[1536,1024]{1,0:T(8,128)(2,1)} async-done(((bf16[384,1024]{1,0:T(8,128)(2,1)}), bf16[1536,1024]{1,0:T(8,128)(2,1)}) %all-gather.7.cloned.1.call-update) | async-done | bytes 3145744 | tf_op jit(solution)/shard_map/all_gather | solution.py:87
  68.1 36.4 %while.28 = (s32[]{:T(128)}, bf16[3,512,2,2,64]{1,4,3,2,0:T(8,128)(2,1)}, f32[3,2,2,512]{3,2,1,0:T(2,128)}, s32[3,512]{1,0:T(4,128)S(1)}, s32[1536]{0:T(1024)S(1...) while((s32[]{:T(128)}, ...), condition=%wide.region_4.5_spmd.clone, body=%wide.region_1.4_spmd.clone.sunk | while | flops 845412352 | bytes 42552428 | solution.py:135
  124.3 30.5 %reduce-scatter.10.cloned.1.call-done = bf16[384,1024]{1,0:T(8,128)(2,1)} async-done(((bf16[1536,1024]{1,0:T(8,128)(2,1)}), bf16[384,1024]{1,0:T(8,128)(2,1)}) %reduce-scatter.10.cloned.1.call-update) | async-done | bytes 786448 | tf_op jit(solution)/shard_map/reduce_scatter | solution.py:137
  160.5 20.3 %scatter_custom_fusion.1 = bf16[4096,1024]{1,0:T(8,128)(2,1)} fusion(s32[3072]{0:T(1024)S(1)} %bitcast.375, f32[384,1024]{1,0:T(8,128)S(1)} %convert_element_type.220, f32[3072]{0:T(1024)S(1)} %div.105, bf16[]{:T(256)} %constant.94.clone.1), kind=kCustom, calls=%fused_computation.111 | custom fusion | flops 6291456 | bytes 9973762 | tf_op jit(solution)/shard_map/scatter | solution.py:192
  187.0 48.3 %scatter_custom_fusion = bf16[4096,1024]{1,0:T(8,128)(2,1)} fusion(s32[3072]{0:T(1024)S(1)} %bitcast.376, bf16[384,1024]{1,0:T(8,128)(2,1)} %copy-done.22, s32[3072]{0:T(1024)S(1)} %broadcast_clamp_fusion.1, bf16[]{:T(256)} %constant.94.clone.1), kind=kCustom, calls=%fused_computation.112 | custom fusion | bytes 8389120 | tf_op jit(solution)/shard_map/scatter | solution.py:162
  235.3 134.5 %all-to-all-done.2 = bf16[4,8,128,1024]{3,2,1,0:T(8,128)(2,1)} async-done(((bf16[4,8,128,1024]{3,2,1,0:T(8,128)(2,1)}), bf16[4,8,128,1024]{3,2,1,0:T(8,128)(2,1)}, u32[]{:S(2)}, u32[]{:S(2)}) %all-to-all-start.2) | async-done | bytes 8388640 | tf_op jit(solution)/shard_map/all_to_all | solution.py:50
  376.3 13.7 fusion.67
  390.0 168.0 %all-to-all-done = bf16[4,8,128,1024]{3,2,1,0:T(8,128)(2,1)} async-done(((bf16[4,8,128,1024]{3,2,1,0:T(8,128)(2,1)}), bf16[4,8,128,1024]{3,2,1,0:T(8,128)(2,1)}, u32[]{:S(2)}, u32[]{:S(2)}) %all-to-all-start) | async-done | bytes 8388640 | tf_op jit(solution)/shard_map/all_to_all | solution.py:50
  558.1 13.5 fusion.60
  571.6 17.9 %fusion.56 = (bf16[4,8,128,512]{3,2,0,1:T(8,128)(2,1)}, bf16[4,8,128,512]{3,2,0,1:T(8,128)(2,1)}, bf16[4,8,128,512]{3,2,0,1:T(8,128)(2,1)}) fusion(f32[8,4,128,512]{3,2,1,0:T(8,128)} %fusion.60, f32[8,4,128,512]{3,2,1,0:T(8,128)} %fusion.67, bf16[8,1024,512]{2,1,0:T(8,128)(2,1)} %all-gather.9.cloned.1.call-done, bf16[4,8,128,1024]{3,2,1,0:T(8,128)(2,1)} %all-to-all-done), kind=kOutput, calls=%fused_computation.81 | convolution fusion | flops 4328521728 | bytes 46137344 | tf_op jit(solution)/shard_map/nlcd,ldf->nlcf/dot_general | solution.py:170
  612.7 16.4 %copy.165 = bf16[64,8,8,1024]{3,1,2,0:T(8,128)(2,1)} copy(bf16[64,8,8,1024]{3,2,1,0:T(8,128)(2,1)} %bitcast.348) | data formatting | bytes 16777216
  652.4 16.6 %copy.167 = bf16[64,8,8,1024]{3,1,2,0:T(8,128)(2,1)} copy(bf16[64,8,8,1024]{3,2,1,0:T(8,128)(2,1)} %bitcast.349) | data formatting | bytes 16777216
  669.1 13.1 convert_bitcast_fusion
  709.2 15.6 %fusion.58 = f32[8,4,128,1024]{3,2,1,0:T(8,128)} fusion(bf16[4,8,128,512]{3,2,0,1:T(8,128)(2,1)} %get-tuple-element.365, bf16[8,1024,512]{2,1,0:T(8,128)(2,1)} %all-gather.11.cloned.1.call-done), kind=kOutput, calls=%fused_computation.83 | convolution fusion | flops 4294967296 | bytes 29360128 | tf_op jit(solution)/shard_map/nlcf,ldf->nlcd/dot_general | solution.py:210
  724.7 16.0 %fusion.57 = bf16[4,8,128,1024]{3,2,0,1:T(8,128)(2,1)} fusion(f32[8,4,128,1024]{3,2,1,0:T(8,128)} %fusion.58, bf16[4,8,128,512]{3,2,0,1:T(8,128)(2,1)} %get-tuple-element.364, bf16[8,1024,512]{2,1,0:T(8,128)(2,1)} %all-gather.9.cloned.1.call-done), kind=kOutput, calls=%fused_computation.82 | convolution fusion | flops 4303355904 | bytes 37748736 | tf_op jit(solution)/shard_map/nlcf,ldf->nlcd/dot_general | solution.py:208
  749.2 129.7 %all-to-all-done.1 = bf16[4,8,128,1024]{3,2,1,0:T(8,128)(2,1)} async-done(((bf16[4,8,128,1024]{3,2,1,0:T(8,128)(2,1)}), bf16[4,8,128,1024]{3,2,1,0:T(8,128)(2,1)}, u32[]{:S(2)}, u32[]{:S(2)}) %all-to-all-start.1) | async-done | bytes 8388640 | tf_op jit(solution)/shard_map/all_to_all | solution.py:54
  884.8 20.8 %gather_fusion = bf16[3072,1024]{1,0:T(8,128)(2,1)} fusion(bf16[4096,1024]{1,0:T(8,128)(2,1)} %bitcast.19, s32[3072]{0:T(1024)S(1)} %broadcast_clamp_fusion), kind=kCustom, calls=%fused_computation.1 | custom fusion | bytes 12595200 | tf_op jit(solution)/shard_map/gather | solution.py:182
  913.6 153.5 %all-to-all-done.3 = bf16[4,8,128,1024]{3,2,1,0:T(8,128)(2,1)} async-done(((bf16[4,8,128,1024]{3,2,1,0:T(8,128)(2,1)}), bf16[4,8,128,1024]{3,2,1,0:T(8,128)(2,1)}, u32[]{:S(2)}, u32[]{:S(2)}) %all-to-all-start.3) | async-done | bytes 8388640 | tf_op jit(solution)/shard_map/all_to_all | solution.py:54
  1067.1 20.4 %gather_fusion.1 = bf16[3072,1024]{1,0:T(8,128)(2,1)} fusion(bf16[4096,1024]{1,0:T(8,128)(2,1)} %bitcast.28, s32[3072]{0:T(1024)S(1)} %broadcast_clamp_fusion), kind=kCustom, calls=%fused_computation.2 | custom fusion | bytes 12595200 | tf_op jit(solution)/shard_map/gather | solution.py:226
  1114.1 28.8 %all-gather.15.cloned.1.call-done = bf16[1536,1024]{1,0:T(8,128)(2,1)} async-done(((bf16[384,1024]{1,0:T(8,128)(2,1)}), bf16[1536,1024]{1,0:T(8,128)(2,1)}) %all-gather.15.cloned.1.call-update) | async-done | bytes 3145744 | tf_op jit(solution)/shard_map/all_gather | solution.py:240
  1153.3 135.6 %while.29 = (s32[]{:T(128)}, f32[1536,2,64]{0,2,1:T(8,128)S(1)}, f32[1536,2,64]{0,2,1:T(8,128)}, f32[3,512,2,2,64]{1,0,4,3,2:T(4,128)}, bf16[3,512,2,2,64]{1,4,3...) while((s32[]{:T(128)}, f32[1536,2,64]{0,2,1:T(8,128)S(1)}, ...), condition=%wide.region_23.24_spmd.clone, body=%wide.region_21.23_spmd.clone.sunk | while | flops 2045048832 | bytes 163770704 | solution.py:282
  1321.6 23.0 %reduce-scatter.12.cloned.1.call-done = bf16[384,1024]{1,0:T(8,128)(2,1)} async-done(((bf16[1536,1024]{1,0:T(8,128)(2,1)}), bf16[384,1024]{1,0:T(8,128)(2,1)}) %reduce-scatter.12.cloned.1.call-update) | async-done | bytes 786448 | tf_op jit(solution)/shard_map/reduce_scatter | solution.py:296
  1355.3 36.5 %all-reduce.18 = (f32[1024]{0:T(1024)}, f32[1024]{0:T(1024)}, f32[1024,32]{0,1:T(8,128)}) all-reduce(bf16[1024]{0:T(1024)(128)(2,1)S(1)} %get-tuple-element.351, bf16[1024]{0:T(1024)(128)(2,1)S(1)} %get-tuple-element.352, bf16[1024,32]{0,1:T(8,128)(2,1)S(1)} %copy-done.49), channel_id=1, replica_groups=mesh['dp'=2,'expert'=4,'tensor'=4] {'dp','expert'}, use_global_device_ids=true, to_apply=%region_28.29 | all-reduce | flops 34816 | bytes 208896 | tf_op jit(solution)/shard_map/psum | solution.py:313
  1396.4 35.6 %all-reduce.15.cloned.1.call-done = (f32[1024,256]{1,0:T(8,128)}, f32[1024,128]{1,0:T(8,128)}, f32[1024,128]{1,0:T(8,128)}, f32[256,1024]{1,0:T(8,128)}) async-done(((f32[1024,256]{1,0:T(8,128)}, f32[1024,128]{1,0:T(8,128)}, f32[1024,128]{1,0:T(8,128)}, f32[256,1024]{1,0:T(8,128)}), (f32[1024,256]{1,0:T(8,128)}, f32[1024,128]{1,0:T(8,128)}, f32[1024,128]{1,0:T(8,128)}, ...) | async-done | bytes 3145744 | tf_op jit(solution)/shard_map/psum | solution.py:313
  (361 shorter events, 422.8 us)
Async XLA Ops:
  7.2 100.8 %copy-start = (bf16[256,1024]{1,0:T(8,128)(2,1)S(1)}, bf16[256,1024]{1,0:T(8,128)(2,1)}, u32[]{:S(2)}) copy-start(bf16[256,1024]{1,0:T(8,128)(2,1)} %param.25) | copy-start | bytes 1572868
  7.2 51.7 %all-gather.7.cloned.1.call-start = ((), (), s32[]{:S(2)}) async-start(), calls=%async_computation.9 | async-start | bytes 3932160 | tf_op jit(solution)/shard_map/all_gather | solution.py:87
  12.1 142.7 %reduce-scatter.10.cloned.1.call-start = ((), (), s32[]{:S(2)}) async-start(), calls=%async_computation.10 | async-start | bytes 3932160 | tf_op jit(solution)/shard_map/reduce_scatter | solution.py:137
  110.7 265.6 %all-gather.13.cloned.1.call-start = ((), (), s32[]{:S(2)}) async-start(), calls=%async_computation.13 | async-start | bytes 10485760 | tf_op jit(solution)/shard_map/all_gather | solution.py:168
  180.8 189.0 %all-to-all-start.2 = ((bf16[4,8,128,1024]{3,2,1,0:T(8,128)(2,1)}), bf16[4,8,128,1024]{3,2,1,0:T(8,128)(2,1)}, u32[]{:S(2)}, u32[]{:S(2)}) async-start(bf16[4,8,128,1024]{3,2,1,0:T(8,128)(2,1)} %bitcast.347), calls=%async_computation.3 | async-start | bytes 16777216 | tf_op jit(solution)/shard_map/all_to_all | solution.py:50
  186.4 203.6 %all-gather.11.cloned.1.call-start = ((), (), s32[]{:S(2)}) async-start(), calls=%async_computation.12 | async-start | bytes 10485760 | tf_op jit(solution)/shard_map/all_gather | solution.py:167
  369.8 188.3 %all-to-all-start = ((bf16[4,8,128,1024]{3,2,1,0:T(8,128)(2,1)}), bf16[4,8,128,1024]{3,2,1,0:T(8,128)(2,1)}, u32[]{:S(2)}, u32[]{:S(2)}) async-start(bf16[4,8,128,1024]{3,2,1,0:T(8,128)(2,1)} %bitcast.346), calls=%async_computation.1 | async-start | bytes 16777216 | tf_op jit(solution)/shard_map/all_to_all | solution.py:50
  375.4 196.2 %all-gather.9.cloned.1.call-start = ((), (), s32[]{:S(2)}) async-start(), calls=%async_computation.11 | async-start | bytes 10485760 | tf_op jit(solution)/shard_map/all_gather | solution.py:166
  376.0 726.3 %reduce-scatter.16.cloned.1.call-start = ((), (), s32[]{:S(2)}) async-start(), calls=%async_computation.18 | async-start | bytes 10485760
  629.1 479.1 %reduce-scatter.18.cloned.1.call-start = ((), (), s32[]{:S(2)}) async-start(), calls=%async_computation.19 | async-start | bytes 10485760
  690.4 188.5 %all-to-all-start.1 = ((bf16[4,8,128,1024]{3,2,1,0:T(8,128)(2,1)}), bf16[4,8,128,1024]{3,2,1,0:T(8,128)(2,1)}, u32[]{:S(2)}, u32[]{:S(2)}) async-start(bf16[4,8,128,1024]{3,2,1,0:T(8,128)(2,1)} %copy.108), calls=%async_computation.2 | async-start | bytes 16777216 | tf_op jit(solution)/shard_map/all_to_all | solution.py:54
  696.1 417.9 %reduce-scatter.14.cloned.1.call-start = ((), (), s32[]{:S(2)}) async-start(), calls=%async_computation.17 | async-start | bytes 10485760 | tf_op jit(solution)/shard_map/reduce_scatter | solution.py:218
  749.2 135.5 %copy-start.59 = (s32[3072,1]{0,1:T(1,128)S(1)}, s32[3072,1]{0,1:T(1,128)}, u32[]{:S(2)}) copy-start(s32[3072,1]{0,1:T(1,128)} %copy-done.58) | copy-start | bytes 36868
  878.9 188.2 %all-to-all-start.3 = ((bf16[4,8,128,1024]{3,2,1,0:T(8,128)(2,1)}), bf16[4,8,128,1024]{3,2,1,0:T(8,128)(2,1)}, u32[]{:S(2)}, u32[]{:S(2)}) async-start(bf16[4,8,128,1024]{3,2,1,0:T(8,128)(2,1)} %copy.111), calls=%async_computation.4 | async-start | bytes 16777216 | tf_op jit(solution)/shard_map/all_to_all | solution.py:54
  884.7 258.2 %all-gather.15.cloned.1.call-start = ((), (), s32[]{:S(2)}) async-start(), calls=%async_computation.14 | async-start | bytes 3932160 | tf_op jit(solution)/shard_map/all_gather | solution.py:240
  1100.7 211.8 %all-reduce.13.cloned.1.call-start = ((), (), s32[]{:S(2)}) async-start(), calls=%async_computation.16 | async-start | bytes 131072 | tf_op jit(solution)/shard_map/psum | solution.py:311
  1102.3 210.3 %all-reduce.17.cloned.1.call-start = ((), (), s32[]{:S(2)}) async-start(), calls=%async_computation.21 | async-start | bytes 12582912 | tf_op jit(solution)/shard_map/psum | solution.py:318
  1114.1 230.6 %reduce-scatter.12.cloned.1.call-start = ((), (), s32[]{:S(2)}) async-start(), calls=%async_computation.15 | async-start | bytes 3932160 | tf_op jit(solution)/shard_map/reduce_scatter | solution.py:296
  1300.7 131.4 %all-reduce.15.cloned.1.call-start = ((), (), s32[]{:S(2)}) async-start(), calls=%async_computation.20 | async-start | bytes 6291456 | tf_op jit(solution)/shard_map/psum | solution.py:313
  1316.7 75.1 %copy-start.66 = (f32[384]{0:T(512)S(1)}, f32[384]{0:T(512)}, u32[]{:S(2)}) copy-start(f32[384]{0:T(512)} %copy-done.65) | copy-start | bytes 4612
  1316.7 75.2 %copy-start.12 = (bf16[384,1024]{1,0:T(8,128)(2,1)S(1)}, bf16[384,1024]{1,0:T(8,128)(2,1)}, u32[]{:S(2)}) copy-start(bf16[384,1024]{1,0:T(8,128)(2,1)} %reduce-scatter.10.cloned.1.call-done) | copy-start | bytes 2359300
  1316.7 75.2 %copy-start.21 = (bf16[384,1024]{1,0:T(8,128)(2,1)S(1)}, bf16[384,1024]{1,0:T(8,128)(2,1)}, u32[]{:S(2)}) copy-start(bf16[384,1024]{1,0:T(8,128)(2,1)} %param.31) | copy-start | bytes 2359300
  1316.7 75.1 %copy-start.52 = (f32[1024]{0:T(1024)S(1)}, f32[1024]{0:T(1024)}, u32[]{:S(2)}) copy-start(f32[1024]{0:T(1024)} %param.26) | copy-start | bytes 12292
  1316.7 75.1 %copy-start.57 = (f32[384]{0:T(512)S(1)}, f32[384]{0:T(512)}, u32[]{:S(2)}) copy-start(f32[384]{0:T(512)} %copy-done.55) | copy-start | bytes 4612
  (76 other events, 1101.4 us)
Sparse Core Ops, SparseCore 0:
  12.2 46.6 all-gather.6
  110.8 43.9 reduce-scatter.9
  156.6 87.5 all-gather.12
  245.9 87.4 all-gather.10
  377.8 87.8 all-gather.8
  629.3 84.5 reduce-scatter.15
  717.2 86.3 reduce-scatter.17
  806.6 86.4 reduce-scatter.13
  1100.8 42.0 all-gather.14
  1146.4 41.4 all-reduce.12
  1191.3 32.2 all-reduce.16
  1300.8 43.8 reduce-scatter.11
  1348.0 83.9 all-reduce.14
where the time goes:
time: 1460 us; the launch traced here: 1450 us
  waiting for transfers between devices  741 us (51%)
  local copies, waits for them, and re-layouts  254 us (17%)
  matrix products  249 us (17%)
  other arithmetic  108 us (7%)
  blocking collectives  54.9 us (4%)
  starting transfers between devices  23.9 us (2%)
  between operations  15.2 us (1%)
    all_to_all x2, waiting for transfers between devices, to_owners(): lax.all_to_all(buffer, 'expert', split_axis=0, concat_axis=0, tiled=True)  303 us
    all_to_all x2, waiting for transfers between devices, to_sources(): lax.all_to_all(buffer, 'expert', split_axis=0, concat_axis=0, tiled=True)  283 us
    unnamed x154, local copies, waits for them, and re-layouts  88.8 us
    scatter x1, local copies, waits for them, and re-layouts, body(): send_rows = jnp.zeros((experts_all * capacity, model_width), jnp.bfloat16...  48.3 us
    psum x1, blocking collectives, body(): lax.psum((query_wgrad, key_wgrad, value_wgrad, out_wgrad, norm_one_grad,...  36.5 us
    all_gather x1, waiting for transfers between devices, body(): lax.all_gather(normed, 'tensor', axis=0, tiled=True)  35.7 us
    psum x1, waiting for transfers between devices, body(): lax.psum((query_wgrad, key_wgrad, value_wgrad, out_wgrad, norm_one_grad,...  35.6 us
    dynamic_update_slice x6, local copies, waits for them, and re-layouts, body(): lax.map(attend, (block_queries, block_places, block_segs))  35 us
  transfers between devices with their start and end apart: 17, of which 9 were waited for; matrix products, arithmetic and copies ran while one was open for 33% of the time, Pallas kernels for 0%

commit v1 on v0

v1 whole, which is shorter than its diff:
```python
import jax
import jax.numpy as jnp
from jax import lax
from jax.sharding import PartitionSpec as P

HEAD = 64
CAP = 128


epsilon = 1e-06
highest = lax.Precision.HIGHEST


def rms_norm(features, gain_vec):
    return (
        features
        * lax.rsqrt(jnp.mean(features * features, axis=-1, keepdims=True) + epsilon)
        * gain_vec
    )


def rotate(vectors, places):
    half_dim = vectors.shape[-1] // 2
    frequency = 10000.0 ** (-jnp.arange(half_dim, dtype=jnp.float32) / half_dim)
    angles = places.astype(jnp.float32)[:, None] * frequency[None, :]
    cosine = jnp.cos(angles)[:, None, :]
    sine_part = jnp.sin(angles)[:, None, :]
    front_half = vectors[..., :half_dim]
    back_half = vectors[..., half_dim:]
    return jnp.concatenate(
        [front_half * cosine - back_half * sine_part, back_half * cosine + front_half * sine_part],
        axis=-1,
    )


def contract_rows(left_in, right_in):
    return lax.dot_general(
        left_in, right_in, (((0,), (0,)), ((), ())), preferred_element_type=jnp.float32
    )


def contract_cols(left_in, right_in):
    return lax.dot_general(
        left_in, right_in, (((1,), (1,)), ((), ())), preferred_element_type=jnp.float32
    )


def gather_over(array, axis_name, dim=0):
    return lax.all_gather(array, axis_name, axis=dim, tiled=True)


def scatter_over(array, axis_name, dim=0):
    return lax.psum_scatter(array, axis_name, scatter_dimension=dim, tiled=True)


def swap_cores(array):
    return lax.ppermute(array, "dp", [(0, 1), (1, 0)])


def own_half(weight):
    half = weight.shape[1] // 2
    return lax.dynamic_slice_in_dim(weight, lax.axis_index("dp") * half, half, axis=1)


def join_halves(mine, theirs):
    first = lax.axis_index("dp") == 0
    return jnp.concatenate(
        [jnp.where(first, mine, theirs), jnp.where(first, theirs, mine)], axis=1
    )


def body(
    tokens,
    segments,
    routes,
    norm_one,
    w_query,
    w_key,
    w_value,
    w_out,
    norm_two,
    w_router,
    w_gate,
    w_up,
    w_down,
    cotangent,
):
    f32, bf16 = jnp.float32, jnp.bfloat16
    local_rows, model_width = tokens.shape
    query_cols, kv_cols = w_query.shape[1], w_key.shape[1]
    head_local, kv_local = query_cols // HEAD, kv_cols // HEAD
    group_size = head_local // kv_local
    expert_local = w_gate.shape[0]
    owner_count = lax.axis_size("expert")
    experts_all = expert_local * owner_count
    score_scale = HEAD ** (-0.5)
    first_expert = lax.axis_index("expert") * expert_local

    inputs = tokens.astype(f32)
    normed_one, norm_back_one = jax.vjp(rms_norm, inputs, norm_one)
    normed = normed_one.astype(bf16)
    normed_all = gather_over(normed, "tensor")
    segs_all = gather_over(segments, "tensor")

    gate_mine = gather_over(own_half(jnp.swapaxes(w_gate, 1, 2)), "tensor", 1)
    up_mine = gather_over(own_half(jnp.swapaxes(w_up, 1, 2)), "tensor", 1)
    down_mine = gather_over(own_half(w_down), "tensor", 1)
    half_units = gate_mine.shape[1]
    units = 2 * half_units
    gate_up = jnp.concatenate(
        [gate_mine, swap_cores(gate_mine), up_mine, swap_cores(up_mine)], axis=1
    )
    down = jnp.concatenate([down_mine, swap_cores(down_mine)], axis=1)

    routes_all = lax.all_gather(routes, "expert", axis=0)
    local_ids = first_expert + jnp.arange(expert_local, dtype=jnp.int32)
    marks = jnp.any(routes_all[:, None, :, :] == local_ids[None, :, None, None], axis=-1)
    order = jnp.arange(local_rows, dtype=jnp.int32)
    earlier = (order[:, None] < order[None, :]).astype(bf16)
    ranks = jnp.einsum("nlt,tu->nlu", marks.astype(bf16), earlier, preferred_element_type=f32)
    places_of = jnp.where(marks, ranks.astype(jnp.int32), -1)
    in_slot = places_of[:, :, None, :] == jnp.arange(CAP, dtype=jnp.int32)[None, None, :, None]
    pick = in_slot.astype(bf16)

    def to_slots(rows_all):
        return jnp.einsum("nlct,ntd->nlcd", pick, rows_all, preferred_element_type=f32).astype(bf16)

    def to_rows(slots):
        return jnp.einsum("nlct,nlcd->ntd", pick, slots, preferred_element_type=f32).astype(bf16)

    up_slots = to_slots(lax.all_gather(cotangent, "expert", axis=0))

    length = normed_all.shape[0]
    places = jnp.arange(length, dtype=jnp.int32)
    w_qkv = jnp.concatenate([w_query, w_key, w_value], axis=1)
    qkv = jnp.dot(normed_all, w_qkv, preferred_element_type=f32)
    query_raw = qkv[:, :query_cols].reshape(length, head_local, HEAD)
    key_raw = qkv[:, query_cols : query_cols + kv_cols].reshape(length, kv_local, HEAD)
    value_rows = qkv[:, query_cols + kv_cols :].astype(bf16).reshape(length, kv_local, HEAD)
    query_turned, rope_query = jax.vjp(lambda vectors: rotate(vectors, places), query_raw)
    key_turned, rope_key = jax.vjp(lambda vectors: rotate(vectors, places), key_raw)
    key_rows = key_turned.astype(bf16)
    queries = query_turned.astype(bf16).reshape(length, kv_local, group_size, HEAD)
    block_count = max(1, length // 512)
    block_rows = length // block_count

    def block_scores(block):
        start, end = block * block_rows, (block + 1) * block_rows
        scores = (
            jnp.einsum(
                "qkgd,skd->kgqs", queries[start:end], key_rows[:end], preferred_element_type=f32
            )
            * score_scale
        )
        allowed = (places[None, :end] <= places[start:end, None]) & (
            segs_all[None, :end] == segs_all[start:end, None]
        )
        return jnp.where(allowed, scores, -1e30)

    mixed_parts, log_totals = [], []
    for block in range(block_count):
        end = (block + 1) * block_rows
        masked = block_scores(block)
        largest = jnp.max(masked, axis=-1, keepdims=True)
        weights = jnp.exp(masked - largest)
        row_total = jnp.sum(weights, axis=-1, keepdims=True)
        prob_rows = (weights / row_total).astype(bf16)
        mixed_parts.append(
            jnp.einsum("kgqs,skd->qkgd", prob_rows, value_rows[:end], preferred_element_type=f32)
            .astype(bf16)
            .reshape(block_rows, query_cols)
        )
        log_totals.append(largest + jnp.log(row_total))
    mixed_heads = jnp.concatenate(mixed_parts, axis=0)
    attention = scatter_over(
        jnp.dot(mixed_heads, w_out, preferred_element_type=f32).astype(bf16), "tensor"
    ).astype(f32)
    hidden = inputs + attention
    normed_two, norm_back_two = jax.vjp(rms_norm, hidden, norm_two)
    routed = normed_two.astype(bf16)
    row_slots = to_slots(lax.all_gather(routed, "expert", axis=0))

    logits = jnp.dot(routed, w_router, preferred_element_type=f32)
    route_onehot = (
        routes[:, :, None] == jnp.arange(experts_all, dtype=jnp.int32)[None, None, :]
    ).astype(f32)
    chosen = jnp.sum(route_onehot * logits[:, None, :], axis=-1)
    gate_probs = jax.nn.softmax(chosen, axis=-1)
    gate_table = jnp.sum(route_onehot * gate_probs[:, :, None], axis=1)
    gates_all = lax.all_to_all(
        gate_table.T.reshape(owner_count, expert_local, local_rows), "expert", 0, 0, tiled=True
    )
    gate_slots = jnp.sum(jnp.where(in_slot, gates_all[:, :, None, :], 0.0), axis=-1)[..., None]

    both_val = jnp.einsum("nlcd,lfd->nlcf", row_slots, gate_up, preferred_element_type=f32)
    gate_val, up_val = both_val[..., :units], both_val[..., units:]
    sigmoid = jax.nn.sigmoid(gate_val)
    silu = gate_val * sigmoid
    inner = silu * up_val
    gated_inner = (gate_slots * inner).astype(bf16)
    down_back = jnp.einsum("nlcd,lfd->nlcf", up_slots, down, preferred_element_type=f32)
    gate_grad_slots = jnp.sum(inner * down_back, axis=-1)
    inner_grad = gate_slots * down_back
    both_back = jnp.concatenate(
        [
            (inner_grad * up_val * (sigmoid * (1.0 + gate_val * (1.0 - sigmoid)))).astype(bf16),
            (inner_grad * silu).astype(bf16),
        ],
        axis=-1,
    )
    row_back = to_rows(
        jnp.einsum("nlcf,lfd->nlcd", both_back, gate_up, preferred_element_type=f32).astype(bf16)
    )
    routed_grad = scatter_over(
        row_back.reshape(owner_count * local_rows, model_width), "expert"
    ).astype(f32)
    gate_grads = lax.all_to_all(
        jnp.sum(jnp.where(in_slot, gate_grad_slots[..., None], 0.0), axis=2),
        "expert",
        0,
        0,
        tiled=True,
    ).reshape(experts_all, local_rows)
    gate_grad = jnp.sum(route_onehot * gate_grads.T[:, None, :], axis=-1)
    expert_rows = to_rows(
        jnp.einsum("nlcf,lfd->nlcd", gated_inner, down, preferred_element_type=f32).astype(bf16)
    )
    block_out = hidden + scatter_over(
        expert_rows.reshape(owner_count * local_rows, model_width), "expert"
    ).astype(f32)

    both_wgrad = jnp.einsum("nlcf,nlcd->lfd", both_back, row_slots, preferred_element_type=f32)
    down_wgrad = jnp.einsum("nlcf,nlcd->lfd", gated_inner, up_slots, preferred_element_type=f32)

    def reduced(wgrad, start):
        theirs = wgrad[:, start + half_units : start + units].astype(bf16)
        total = wgrad[:, start : start + half_units].astype(bf16) + swap_cores(theirs)
        part = scatter_over(total, "tensor", 1)
        return join_halves(part, swap_cores(part)).astype(f32)

    gate_out = jnp.swapaxes(reduced(both_wgrad, 0), 1, 2)
    up_out = jnp.swapaxes(reduced(both_wgrad, units), 1, 2)
    down_out = reduced(down_wgrad, 0)

    upstream = cotangent.astype(f32)
    chosen_grad = gate_probs * (gate_grad - jnp.sum(gate_probs * gate_grad, axis=-1, keepdims=True))
    logit_grad = jnp.sum(route_onehot * chosen_grad[:, :, None], axis=1)
    routed_grad = routed_grad + lax.dot_general(
        logit_grad, w_router.astype(f32), (((1,), (1,)), ((), ())), precision=highest
    )
    router_grad = lax.dot_general(
        routed.astype(f32), logit_grad, (((0,), (0,)), ((), ())), precision=highest
    )
    hidden_part, norm_two_grad = norm_back_two(routed_grad)
    hidden_grad = upstream + hidden_part
    attn_all = gather_over(hidden_grad.astype(bf16), "tensor")
    router_grad, norm_two_grad = lax.psum(
        (router_grad, norm_two_grad), ("dp", "expert", "tensor")
    )
    out_wgrad = lax.psum(contract_rows(mixed_heads, attn_all).astype(bf16), ("dp", "expert"))
    mixed_grad = (
        contract_cols(attn_all, w_out).astype(bf16).reshape(length, kv_local, group_size, HEAD)
    )
    key_parts = [0.0] * block_count
    value_parts = [0.0] * block_count
    query_parts = []
    for block in range(block_count):
        start, end = block * block_rows, (block + 1) * block_rows
        grad_block = mixed_grad[start:end]
        prob_full = jnp.exp(block_scores(block) - log_totals[block])
        prob_grad = jnp.einsum(
            "qkgd,skd->kgqs", grad_block, value_rows[:end], preferred_element_type=f32
        )
        value_grad = jnp.einsum(
            "kgqs,qkgd->skd", prob_full.astype(bf16), grad_block, preferred_element_type=f32
        )
        centred = jnp.sum(prob_full * prob_grad, axis=-1, keepdims=True)
        score_grad = (prob_full * (prob_grad - centred)).astype(bf16)
        query_parts.append(
            jnp.einsum("kgqs,skd->qkgd", score_grad, key_rows[:end], preferred_element_type=f32)
            * score_scale
        )
        key_grad = (
            jnp.einsum("kgqs,qkgd->skd", score_grad, queries[start:end], preferred_element_type=f32)
            * score_scale
        )
        for part in range(block + 1):
            rows = slice(part * block_rows, (part + 1) * block_rows)
            key_parts[part] = key_parts[part] + key_grad[rows]
            value_parts[part] = value_parts[part] + value_grad[rows]
    (query_raw_grad,) = rope_query(
        jnp.concatenate(query_parts, axis=0).reshape(length, head_local, HEAD)
    )
    (key_raw_grad,) = rope_key(jnp.concatenate(key_parts, axis=0))
    qkv_low = jnp.concatenate(
        [
            query_raw_grad.reshape(length, query_cols).astype(bf16),
            key_raw_grad.reshape(length, kv_cols).astype(bf16),
            jnp.concatenate(value_parts, axis=0).reshape(length, kv_cols).astype(bf16),
        ],
        axis=1,
    )
    normed_grad = scatter_over(contract_cols(qkv_low, w_qkv).astype(bf16), "tensor").astype(f32)
    qkv_wgrad = lax.psum(
        contract_rows(normed_all, qkv_low).astype(bf16), ("dp", "expert")
    ).astype(f32)
    input_part, norm_one_grad = norm_back_one(normed_grad)
    norm_one_grad = lax.psum(norm_one_grad, ("dp", "expert", "tensor"))
    return (
        block_out.astype(bf16),
        hidden_grad + input_part,
        norm_one_grad,
        qkv_wgrad[:, :query_cols],
        qkv_wgrad[:, query_cols : query_cols + kv_cols],
        qkv_wgrad[:, query_cols + kv_cols :],
        out_wgrad.astype(f32),
        norm_two_grad,
        router_grad,
        gate_out,
        up_out,
        down_out,
    )


def solution(mesh):
    placed = (
        P(("dp", "expert", "tensor"), None),
        P(("dp", "expert", "tensor")),
        P(("dp", "expert", "tensor"), None),
        P(),
        P(None, "tensor"),
        P(None, "tensor"),
        P(None, "tensor"),
        P("tensor", None),
        P(),
        P(),
        P("expert", None, "tensor"),
        P("expert", None, "tensor"),
        P("expert", "tensor", None),
        P(("dp", "expert", "tensor"), None),
    )
    return jax.shard_map(
        body,
        mesh=mesh,
        in_specs=placed,
        out_specs=(
            P(("dp", "expert", "tensor"), None),
            P(("dp", "expert", "tensor"), None),
            P(),
            P(None, "tensor"),
            P(None, "tensor"),
            P(None, "tensor"),
            P("tensor", None),
            P(),
            P(),
            P("expert", None, "tensor"),
            P("expert", None, "tensor"),
            P("expert", "tensor", None),
        ),
        check_vma=False,
    )
```

time: 1460 us -> 1090 us (0.75)
  local copies, waits for them, and re-layouts: 254 us -> 72.5 us
  waiting for transfers between devices: 741 us -> 635 us
  matrix products: 249 us -> 187 us
  other arithmetic: 108 us -> 92.7 us
    all_to_all x4 -> x2, waiting for transfers between devices: 586 us -> 0.01 us  [the longest x1 0.01 us: body(): lax.all_to_all(gate_table.T.reshape(owner_count, expert_local, local_rows...]
    all_gather x5 -> x7, waiting for transfers between devices: 64.5 us -> 240 us  [the longest x5 153 us: gather_over(): return lax.all_gather(array, axis_name, axis=dim, tiled=True)]
    reduce_scatter x3 -> x7, waiting for transfers between devices: 53.5 us -> 206 us  [scatter_over(): return lax.psum_scatter(array, axis_name, scatter_dimension=dim, tiled=True)]
    psum x3 -> x2, waiting for transfers between devices: 35.7 us -> 179 us  [the longest x1 115 us: body(): lax.psum((router_grad, norm_two_grad), ('dp', 'expert', 'tensor'))]
    dot_general x37 -> x32, matrix products: 229 us -> 174 us  [the longest x2 32.1 us: to_rows(): jnp.einsum('nlct,nlcd->ntd', pick, slots, preferred_element_type=f32)]
    scatter x1 -> x0, local copies, waits for them, and re-layouts: 48.3 us -> none  [body(): send_rows = jnp.zeros((experts_all * capacity, model_width), jnp.bfloat16...]
    unnamed x154 -> x209, local copies, waits for them, and re-layouts: 88.8 us -> 47.2 us
    gather x2 -> x0, local copies, waits for them, and re-layouts: 41.2 us -> none  [the longest x1 20.8 us: body(): returned[slot_index].reshape(local_rows, TOP, model_width)]
  transfers between devices with their start and end apart: 17 -> 27, of which waited for: 9 -> 16; matrix products, arithmetic and copies ran while one was open for 33% -> 27% of each run, Pallas kernels for 0% -> 0%
where the time goes in v1:
time: 1090 us; the launch traced here: 1080 us
  waiting for transfers between devices  635 us (58%)
  matrix products  187 us (17%)
  other arithmetic  92.7 us (9%)
  local copies, waits for them, and re-layouts  72.5 us (7%)
  blocking collectives  67.3 us (6%)
  between operations  15.9 us (1%)
    reduce_scatter x7, waiting for transfers between devices, scatter_over(): return lax.psum_scatter(array, axis_name, scatter_dimension=dim, tiled=True)  206 us
    all_gather x5, waiting for transfers between devices, gather_over(): return lax.all_gather(array, axis_name, axis=dim, tiled=True)  153 us
    psum x1, waiting for transfers between devices, body(): lax.psum((router_grad, norm_two_grad), ('dp', 'expert', 'tensor'))  115 us
    psum x1, waiting for transfers between devices, body(): lax.psum(contract_rows(normed_all, qkv_low).astype(bf16), ('dp', 'expert'))  63.5 us
    all_gather x1, waiting for transfers between devices, body(): up_slots = to_slots(lax.all_gather(cotangent, 'expert', axis=0))  47.5 us
    unnamed x209, local copies, waits for them, and re-layouts  47.2 us
    psum x1, blocking collectives, body(): norm_one_grad = lax.psum(norm_one_grad, ('dp', 'expert', 'tensor'))  44.2 us
    all_gather x1, waiting for transfers between devices, body(): row_slots = to_slots(lax.all_gather(routed, 'expert', axis=0))  38.8 us
  transfers between devices with their start and end apart: 27, of which 16 were waited for; matrix products, arithmetic and copies ran while one was open for 27% of the time, Pallas kernels for 0%

profile of v1, /device:TPU:0, one launch (start us, length us, event | category | flops | bytes accessed | tf_op | source)
XLA Modules:
  0.0 1079.8 jit_solution(6974283397293371100)
XLA Ops:
  41.1 18.0 %all-gather.12.cloned.1.call-done = bf16[1536,1024]{1,0:T(8,128)(2,1)} async-done(((bf16[384,1024]{1,0:T(8,128)(2,1)}), bf16[1536,1024]{1,0:T(8,128)(2,1)}) %all-gather.12.cloned.1.call-update) | async-done | bytes 3145744 | tf_op jit(solution)/shard_map/all_gather | solution.py:49
  91.0 23.3 %all-gather.16.cloned.1.call-done = bf16[8,256,1024]{2,1,0:T(8,128)(2,1)} async-done(((bf16[8,64,1024]{2,1,0:T(8,128)(2,1)}), bf16[8,256,1024]{2,1,0:T(8,128)(2,1)}) %all-gather.16.cloned.1.call-update) | async-done | bytes 4194320 | tf_op jit(solution)/shard_map/all_gather | solution.py:49
  114.2 55.2 %all-gather.18.cloned.1.call-done = bf16[8,256,1024]{2,1,0:T(8,128)(2,1)} async-done(((bf16[8,64,1024]{2,1,0:T(8,128)(2,1)}), bf16[8,256,1024]{2,1,0:T(8,128)(2,1)}) %all-gather.18.cloned.1.call-update) | async-done | bytes 4194320 | tf_op jit(solution)/shard_map/all_gather | solution.py:49
  169.4 47.4 %reduce-scatter.8.cloned.1.call-done = bf16[384,1024]{1,0:T(8,128)(2,1)} async-done(((bf16[1536,1024]{1,0:T(8,128)(2,1)}), bf16[384,1024]{1,0:T(8,128)(2,1)}) %reduce-scatter.8.cloned.1.call-update) | async-done | bytes 786448 | tf_op jit(solution)/shard_map/reduce_scatter | solution.py:53
  220.7 13.5 %all-gather = s32[1536,8]{0,1:T(8,128)S(1)} all-gather(s32[384,8]{0,1:T(8,128)S(1)} %copy-done.52), channel_id=2, replica_groups=mesh['dp'=2,'expert'=4,'tensor'=4] {'expert'}, dimensions={0}, use_global_device_ids=true | all-gather | bytes 61440 | tf_op jit(solution)/shard_map/all_gather | solution.py:115
  234.6 47.5 %all-gather.24.cloned.1.call-done = bf16[1536,1024]{1,0:T(8,128)(2,1)} async-done(((bf16[384,1024]{1,0:T(8,128)(2,1)}), bf16[1536,1024]{1,0:T(8,128)(2,1)}) %all-gather.24.cloned.1.call-update) | async-done | bytes 3145744 | tf_op jit(solution)/shard_map/all_gather | solution.py:131
  292.3 43.2 %all-gather.14.cloned.1.call-done = bf16[8,256,1024]{2,0,1:T(8,128)(2,1)} async-done(((bf16[8,64,1024]{2,0,1:T(8,128)(2,1)}), bf16[8,256,1024]{2,0,1:T(8,128)(2,1)}) %all-gather.14.cloned.1.call-update) | async-done | bytes 4194320 | tf_op jit(solution)/shard_map/all_gather | solution.py:49
  363.3 38.8 %all-gather.22.cloned.1.call-done = bf16[1536,1024]{1,0:T(8,128)(2,1)} async-done(((bf16[384,1024]{1,0:T(8,128)(2,1)}), bf16[1536,1024]{1,0:T(8,128)(2,1)}) %all-gather.22.cloned.1.call-update) | async-done | bytes 3145744 | tf_op jit(solution)/shard_map/all_gather | solution.py:181
  402.2 10.4 convolution_convert_fusion.1
  412.5 18.6 %fusion.9 = f32[4,8,128,1024]{2,3,0,1:T(8,128)} fusion(bf16[8,1024,1024]{2,1,0:T(8,128)(2,1)} %copy-done.41, bf16[4,8,128,1024]{3,2,1,0:T(8,128)(2,1)} %convolution_convert_fusion.1), kind=kOutput, calls=%fused_computation.17 | convolution fusion | flops 8589934592 | bytes 41943040 | tf_op jit(solution)/shard_map/nlcd,lfd->nlcf/dot_general | solution.py:195
  431.1 19.0 %fusion.20 = (f32[4,8,128]{2,0,1:T(4,128)S(1)}, f32[8,512,4,128]{3,1,2,0:T(8,128)}) fusion(f32[4,8,128,1024]{2,3,0,1:T(8,128)} %fusion.9, bf16[4,8,128,1024]{3,2,1,0:T(8,128)(2,1)} %convolution_convert_fusion, bf16[8,256,1024]{1,2,0:T(8,128)(2,1)} %collective-permute-done, bf16[8,256,1024]{1,2,0:T(8,128)(2,1)S(1)} %copy-done.24), kind=kOutput, calls=%fused_computation.32 | convolution fusion | flops 4326420480 | bytes 41959424 | tf_op jit(solution)/shard_map/nlcd,lfd->nlcf/dot_general | solution.py:201
  456.9 14.3 %multiply_convert_fusion.1 = (bf16[4,8,128,512]{2,3,0,1:T(8,128)(2,1)}, bf16[4,8,128,512]{2,3,0,1:T(8,128)(2,1)}, bf16[4,8,128,512]{2,3,0,1:T(8,128)(2,1)}) fusion(f32[8,512,4,128]{3,1,2,0:T(8,128)} %get-tuple-element.127, f32[4,8,128,1024]{2,3,0,1:T(8,128)} %fusion.9, f32[4,8,128]{2,0,1:T(4,128)S(1)} %copy.155), kind=kLoop, calls=%fused_computation.41 | loop fusion | flops 35651584 | bytes 37765120 | tf_op jit(solution)/shard_map/convert_element_type | solution.py:206
  471.2 18.8 %bitcast_convert_fusion.2 = bf16[4,384,1024]{2,1,0:T(8,128)(2,1)} fusion(s32[4,8,384]{2,1,0:T(8,128)S(1)} %fusion.118, bf16[8,1024,1024]{2,1,0:T(8,128)(2,1)} %copy-done.41, bf16[4,8,128,512]{2,3,0,1:T(8,128)(2,1)} %get-tuple-element.83, bf16[4,8,128,512]{2,3,0,1:T(8,128)(2,1)} %get-tuple-element.82), kind=kOutput, calls=%fused_computation.58 | convolution fusion | flops 11835277312 | bytes 28360704 | tf_op jit(solution)/shard_map/nlct,nlcd->ntd/dot_general | solution.py:129
  493.3 17.2 %bitcast_convert_fusion = bf16[8,1024,1024]{2,1,0:T(8,128)(2,1)} fusion(bf16[4,8,128,1024]{3,2,1,0:T(8,128)(2,1)} %convolution_convert_fusion.1, bf16[4,8,128,512]{2,3,0,1:T(8,128)(2,1)} %get-tuple-element.83, bf16[4,8,128,512]{2,3,0,1:T(8,128)(2,1)} %get-tuple-element.82), kind=kOutput, calls=%fused_computation | convolution fusion | flops 8615100416 | bytes 33554432 | tf_op jit(solution)/shard_map/nlcf,nlcd->lfd/dot_general | solution.py:232
  515.5 33.7 %reduce-scatter.12.cloned.1.call-done = bf16[384,1024]{1,0:T(8,128)(2,1)} async-done(((bf16[1536,1024]{1,0:T(8,128)(2,1)}), bf16[384,1024]{1,0:T(8,128)(2,1)}) %reduce-scatter.12.cloned.1.call-update) | async-done | bytes 786448 | tf_op jit(solution)/shard_map/reduce_scatter | solution.py:53
  585.8 13.6 %all-gather.20.cloned.1.call-done = bf16[1536,1024]{1,0:T(8,128)(2,1)} async-done(((bf16[384,1024]{1,0:T(8,128)(2,1)}), bf16[1536,1024]{1,0:T(8,128)(2,1)}) %all-gather.20.cloned.1.call-update) | async-done | bytes 3145744 | tf_op jit(solution)/shard_map/all_gather | solution.py:49
  670.7 13.3 %bitcast_convert_fusion.3 = bf16[4,384,1024]{2,1,0:T(8,128)(2,1)} fusion(bf16[8,256,1024]{1,2,0:T(8,128)(2,1)} %collective-permute-done, bf16[8,256,1024]{1,2,0:T(8,128)(2,1)} %copy.154, bf16[4,8,128,512]{2,3,0,1:T(8,128)(2,1)} %get-tuple-element.84, s32[4,8,384]{2,1,0:T(8,128)S(1)} %copy-done.59), kind=kOutput, calls=%fused_computation.59 | convolution fusion | flops 7540310016 | bytes 15777792 | tf_op jit(solution)/shard_map/nlct,nlcd->ntd/dot_general | solution.py:129
  684.4 27.1 %reduce-scatter.20.cloned.1.call-done = bf16[8,64,1024]{2,1,0:T(8,128)(2,1)} async-done(((bf16[8,256,1024]{2,1,0:T(8,128)(2,1)}), bf16[8,64,1024]{2,1,0:T(8,128)(2,1)}) %reduce-scatter.20.cloned.1.call-update) | async-done | bytes 1048592 | tf_op jit(solution)/shard_map/reduce_scatter | solution.py:53
  712.6 63.5 %all-reduce.11.cloned.1.call-done = (bf16[1024,512]{1,0:T(8,128)(2,1)}, bf16[256,1024]{1,0:T(8,128)(2,1)}) async-done(((bf16[1024,512]{1,0:T(8,128)(2,1)}, bf16[256,1024]{1,0:T(8,128)(2,1)}), (bf16[1024,512]{1,0:T(8,128)(2,1)}, bf16[256,1024]{1,0:T(8,128)(2,1)})) %all-reduce.11.cloned.1.call-update) | async-done | bytes 1572880 | tf_op jit(solution)/shard_map/psum | solution.py:304
  793.8 37.4 %reduce-scatter.16.cloned.1.call-done = bf16[8,64,1024]{2,1,0:T(8,128)(2,1)} async-done(((bf16[8,256,1024]{2,1,0:T(8,128)(2,1)}), bf16[8,64,1024]{2,1,0:T(8,128)(2,1)}) %reduce-scatter.16.cloned.1.call-update) | async-done | bytes 1048592 | tf_op jit(solution)/shard_map/reduce_scatter | solution.py:53
  835.2 43.0 %reduce-scatter.14.cloned.1.call-done = bf16[384,1024]{1,0:T(8,128)(2,1)} async-done(((bf16[1536,1024]{1,0:T(8,128)(2,1)}), bf16[384,1024]{1,0:T(8,128)(2,1)}) %reduce-scatter.14.cloned.1.call-update) | async-done | bytes 786448 | tf_op jit(solution)/shard_map/reduce_scatter | solution.py:53
  880.0 44.2 %all-reduce.4 = (f32[1024]{0:T(1024)}, f32[1024]{0:T(1024)}) all-reduce(f32[1024]{0:T(1024)S(1)} %get-tuple-element.74, f32[1024]{0:T(1024)S(1)} %copy-done.81), channel_id=1, replica_groups=mesh['dp'=2,'expert'=4,'tensor'=4] {'dp','expert','tensor'}, use_global_device_ids=true, to_apply=%region_29.30 | all-reduce | flops 2048 | bytes 16384 | tf_op jit(solution)/shard_map/psum | solution.py:308
  924.2 17.6 %reduce-scatter.10.cloned.1.call-done = bf16[384,1024]{1,0:T(8,128)(2,1)} async-done(((bf16[1536,1024]{1,0:T(8,128)(2,1)}), bf16[384,1024]{1,0:T(8,128)(2,1)}) %reduce-scatter.10.cloned.1.call-update) | async-done | bytes 786448 | tf_op jit(solution)/shard_map/reduce_scatter | solution.py:53
  955.7 115.5 %all-reduce.9.cloned.1.call-done = f32[1024,32]{0,1:T(8,128)} async-done(((f32[1024,32]{0,1:T(8,128)}), f32[1024,32]{0,1:T(8,128)}) %all-reduce.9.cloned.1.call-update) | async-done | bytes 131088 | tf_op jit(solution)/shard_map/psum | solution.py:257
  (381 shorter events, 269.8 us)
Async XLA Ops:
  7.2 51.9 %all-gather.12.cloned.1.call-start = ((), (), s32[]{:S(2)}) async-start(), calls=%async_computation.9 | async-start | bytes 3932160 | tf_op jit(solution)/shard_map/all_gather | solution.py:49
  12.2 102.0 %all-gather.16.cloned.1.call-start = ((), (), s32[]{:S(2)}) async-start(), calls=%async_computation.12 | async-start | bytes 5242880 | tf_op jit(solution)/shard_map/all_gather | solution.py:49
  20.5 148.9 %all-gather.18.cloned.1.call-start = ((), (), s32[]{:S(2)}) async-start(), calls=%async_computation.13 | async-start | bytes 5242880 | tf_op jit(solution)/shard_map/all_gather | solution.py:49
  23.4 193.4 %reduce-scatter.8.cloned.1.call-start = ((), (), s32[]{:S(2)}) async-start(), calls=%async_computation.10 | async-start | bytes 3932160 | tf_op jit(solution)/shard_map/reduce_scatter | solution.py:53
  88.6 193.4 %all-gather.24.cloned.1.call-start = ((), (), s32[]{:S(2)}) async-start(), calls=%async_computation.23 | async-start | bytes 3932160 | tf_op jit(solution)/shard_map/all_gather | solution.py:131
  89.2 246.3 %all-gather.14.cloned.1.call-start = ((), (), s32[]{:S(2)}) async-start(), calls=%async_computation.11 | async-start | bytes 5242880 | tf_op jit(solution)/shard_map/all_gather | solution.py:49
  90.9 311.2 %all-gather.22.cloned.1.call-start = ((), (), s32[]{:S(2)}) async-start(), calls=%async_computation.22 | async-start | bytes 3932160 | tf_op jit(solution)/shard_map/all_gather | solution.py:181
  114.2 230.8 %collective-permute-start.1 = (bf16[8,256,1024]{2,1,0:T(8,128)(2,1)}, bf16[8,256,1024]{2,1,0:T(8,128)(2,1)}, u32[]{:S(2)}, u32[]{:S(2)}) collective-permute-start(bf16[8,256,1024]{2,1,0:T(8,128)(2,1)} %all-gather.16.cloned.1.call-done), channel_id=1, source_target_pairs={{0,16},{16,0},{1,17},{17,1},{2,18},{18,2},{3,19},{19,3},{4,20},{20... | collective-permute-start | bytes 12582920 | tf_op jit(solution)/shard_map/ppermute | solution.py:57
  169.4 179.9 %collective-permute-start.2 = (bf16[8,256,1024]{2,1,0:T(8,128)(2,1)}, bf16[8,256,1024]{2,1,0:T(8,128)(2,1)}, u32[]{:S(2)}, u32[]{:S(2)}) collective-permute-start(bf16[8,256,1024]{2,1,0:T(8,128)(2,1)} %all-gather.18.cloned.1.call-done), channel_id=1, source_target_pairs={{0,16},{16,0},{1,17},{17,1},{2,18},{18,2},{3,19},{19,3},{4,20},{20... | collective-permute-start | bytes 12582920 | tf_op jit(solution)/shard_map/ppermute | solution.py:57
  342.3 88.8 %collective-permute-start = (bf16[8,256,1024]{1,2,0:T(8,128)(2,1)}, bf16[8,256,1024]{1,2,0:T(8,128)(2,1)}, u32[]{:S(2)}, u32[]{:S(2)}) collective-permute-start(bf16[8,256,1024]{1,2,0:T(8,128)(2,1)} %copy.154), channel_id=1, source_target_pairs={{0,16},{16,0},{1,17},{17,1},{2,18},{18,2},{3,19},{19,3},{4,20},{20... | collective-permute-start | bytes 12582920 | tf_op jit(solution)/shard_map/ppermute | solution.py:57
  358.7 91.5 %all-to-all-start = ((f32[4,8,384]{2,1,0:T(8,128)}), f32[4,8,384]{2,1,0:T(8,128)S(1)}, u32[]{:S(2)}, u32[]{:S(2)}) async-start(f32[4,8,384]{2,1,0:T(8,128)} %bitcast.33), calls=%async_computation.1 | async-start | bytes 98304 | tf_op jit(solution)/shard_map/all_to_all | solution.py:190
  363.3 185.9 %reduce-scatter.12.cloned.1.call-start = ((), (), s32[]{:S(2)}) async-start(), calls=%async_computation.15 | async-start | bytes 3932160 | tf_op jit(solution)/shard_map/reduce_scatter | solution.py:53
  493.3 106.1 %all-gather.20.cloned.1.call-start = ((), (), s32[]{:S(2)}) async-start(), calls=%async_computation.16 | async-start | bytes 3932160 | tf_op jit(solution)/shard_map/all_gather | solution.py:49
  555.1 129.0 %reduce-scatter.18.cloned.1.call-start = ((), (), s32[]{:S(2)}) async-start(), calls=%async_computation.20 | async-start | bytes 5242880 | tf_op jit(solution)/shard_map/reduce_scatter | solution.py:53
  563.4 148.1 %reduce-scatter.20.cloned.1.call-start = ((), (), s32[]{:S(2)}) async-start(), calls=%async_computation.21 | async-start | bytes 5242880 | tf_op jit(solution)/shard_map/reduce_scatter | solution.py:53
  573.4 85.4 %collective-permute-start.3 = (bf16[8,256,1024]{2,1,0:T(8,128)(2,1)}, bf16[8,256,1024]{2,1,0:T(8,128)(2,1)}, u32[]{:S(2)}, u32[]{:S(2)}) collective-permute-start(bf16[8,256,1024]{2,1,0:T(8,128)(2,1)} %get-tuple-element.86), channel_id=1, source_target_pairs={{0,16},{16,0},{1,17},{17,1},{2,18},{18,2},{3,19},{19,3},{4,20},{20... | collective-permute-start | bytes 12582920 | tf_op jit(solution)/shard_map/ppermute | solution.py:57
  585.8 190.4 %all-reduce.11.cloned.1.call-start = ((), (), s32[]{:S(2)}) async-start(), calls=%async_computation.24 | async-start | bytes 3145728 | tf_op jit(solution)/shard_map/psum | solution.py:304
  658.7 172.5 %reduce-scatter.16.cloned.1.call-start = ((), (), s32[]{:S(2)}) async-start(), calls=%async_computation.19 | async-start | bytes 5242880 | tf_op jit(solution)/shard_map/reduce_scatter | solution.py:53
  664.7 213.5 %reduce-scatter.14.cloned.1.call-start = ((), (), s32[]{:S(2)}) async-start(), calls=%async_computation.17 | async-start | bytes 3932160 | tf_op jit(solution)/shard_map/reduce_scatter | solution.py:53
  670.6 271.2 %reduce-scatter.10.cloned.1.call-start = ((), (), s32[]{:S(2)}) async-start(), calls=%async_computation.14 | async-start | bytes 3932160 | tf_op jit(solution)/shard_map/reduce_scatter | solution.py:53
  684.0 387.2 %all-reduce.9.cloned.1.call-start = ((), (), s32[]{:S(2)}) async-start(), calls=%async_computation.18 | async-start | bytes 262144 | tf_op jit(solution)/shard_map/psum | solution.py:257
  684.1 97.5 %collective-permute-start.6 = (bf16[8,64,1024]{2,1,0:T(8,128)(2,1)}, bf16[8,64,1024]{2,1,0:T(8,128)(2,1)}, u32[]{:S(2)}, u32[]{:S(2)}) collective-permute-start(bf16[8,64,1024]{2,1,0:T(8,128)(2,1)} %reduce-scatter.18.cloned.1.call-done), channel_id=1, source_target_pairs={{0,16},{16,0},{1,17},{17,1},{2,18},{18,2},{3,19},{19,3},{4,20},{20... | collective-permute-start | bytes 3145736 | tf_op jit(solution)/shard_map/ppermute | solution.py:57
  711.5 79.4 %collective-permute-start.8 = (bf16[8,64,1024]{2,1,0:T(8,128)(2,1)}, bf16[8,64,1024]{2,1,0:T(8,128)(2,1)}, u32[]{:S(2)}, u32[]{:S(2)}) collective-permute-start(bf16[8,64,1024]{2,1,0:T(8,128)(2,1)} %reduce-scatter.20.cloned.1.call-done), channel_id=1, source_target_pairs={{0,16},{16,0},{1,17},{17,1},{2,18},{18,2},{3,19},{19,3},{4,20},{20... | collective-permute-start | bytes 3145736 | tf_op jit(solution)/shard_map/ppermute | solution.py:57
  831.2 115.4 %collective-permute-start.4 = (bf16[8,64,1024]{2,1,0:T(8,128)(2,1)}, bf16[8,64,1024]{2,1,0:T(8,128)(2,1)}, u32[]{:S(2)}, u32[]{:S(2)}) collective-permute-start(bf16[8,64,1024]{2,1,0:T(8,128)(2,1)} %reduce-scatter.16.cloned.1.call-done), channel_id=1, source_target_pairs={{0,16},{16,0},{1,17},{17,1},{2,18},{18,2},{3,19},{19,3},{4,20},{20... | collective-permute-start | bytes 3145736 | tf_op jit(solution)/shard_map/ppermute | solution.py:57
  (101 other events, 3030.1 us)
Sparse Core Ops, SparseCore 0:
  12.3 46.7 all-gather.11
  61.5 52.6 all-gather.15
  116.7 52.6 all-gather.17
  172.8 43.9 reduce-scatter.7
  218.2 63.7 all-gather.23
  284.3 51.1 all-gather.13
  337.6 64.4 all-gather.21
  490.1 59.0 reduce-scatter.11
  555.3 44.0 all-gather.19
  602.8 52.6 reduce-scatter.17
  658.7 52.6 reduce-scatter.19
  714.3 61.7 all-reduce.10
  779.1 52.0 reduce-scatter.15
  834.3 43.8 reduce-scatter.13
  880.5 61.2 reduce-scatter.9
  948.7 122.4 all-reduce.8
